TPU v7x, 32 devices: a whole 2x2x4 slice. The times are simulated.
32 devices in a mesh: slab: 4 (over y, x), fsdp: 8 (over z, core).
Axes of the slice: x: 2, y: 2, z: 4, core: 2. Of those that a mesh axis runs over, the one named last changes fastest.
Arguments:
- volume: bfloat16 [128, 128, 128], P('slab'), may hold values from -6 to 6
- noise: bfloat16 [128, 128, 128], P('slab'), may hold values from -6 to 6
- cotangent: bfloat16 [128, 128, 128], P('slab'), may hold values from -1.5 to 1.5
- patch_corner: int32 [4, 32, 3], P('slab'), may hold values from 0 to 96, as said below
- patch_count: int32 [4, 8], P('slab'), may hold values from 0 to 4, as said below
- patch_level: int32 [4, 32], P('slab'), may hold values from 0 to 999
- embed: bfloat16 [512, 2048], replicated, may hold values from -0.25 to 0.25
- unembed: bfloat16 [2048, 512], replicated, may hold values from -0.125 to 0.125
- level_table: bfloat16 [1000, 2048], replicated, may hold values from -6 to 6
- pos_embed: bfloat16 [256, 2048], replicated, may hold values from -3 to 3
- w_qkv: bfloat16 [2048, 3072], P('fsdp'), may hold values from -0.125 to 0.125
- w_out: bfloat16 [1024, 2048], P('fsdp'), may hold values from -0.1875 to 0.1875
Outputs:
- score: float32 [128, 128, 128], P('slab', 'fsdp')
- grad_qk: float32 [2048, 2048], P('fsdp', 'slab')
- grad_v: float32 [2048, 1024], P('fsdp', 'slab')
- grad_out: float32 [1024, 2048], P('fsdp', 'slab')
Inputs may be any that keep to these rules, and one draw needn't show every extreme that they name: patch_corner[s, j] holds multiples of 8; z lies in slab s (s * 32 <= z < (s + 1) * 32) and z + 32 <= 128; y and x are at most 64; entries of slots that are not live are of the same form; the smallest and largest values are reached. `patch_count`: each slab's counts add up to exactly 16; in every slab some device has 4 live slots.
All inputs are finite; a program needn't handle non-finite values.
Results may differ from a plain program's by a relative error of at most 0.024.
Values may be sent and summed in bfloat16 or wider, within the bound.
No kernel may reach another device: no remote copies, remote signals or barrier semaphores. Data moves between devices by JAX's collectives and lax.ppermute only.
A program may use at most 128 MiB of HBM per device.

v0:
```python
import jax
import jax.numpy as jnp
from jax import lax
from jax.sharding import PartitionSpec as P

HD = 128
NLEV = 1000
EDGE = 8
PXY = 8
PZT = 4
PPD = 2
HALO = 24


def from_behind(block, axis, distance):
    devices = range(lax.axis_size(axis))
    route = [(i - distance, i) for i in devices if i - distance in devices]
    return lax.ppermute(block, axis, route)


def layer_normal(hidden):
    centre = hidden - jnp.mean(hidden, axis=-1, keepdims=True)
    inverse = lax.rsqrt(jnp.mean(centre * centre, axis=-1, keepdims=True) + 1e-05)
    return (centre * inverse, inverse)


def head_normal(values):
    inverse = lax.rsqrt(jnp.mean(values * values, axis=-1, keepdims=True) + 1e-06)
    return (values * inverse, inverse)


def contract(form, left, right):
    return jnp.einsum(form, left, right, preferred_element_type=jnp.float32)


def pick_patches(counts, corners, levels, member):
    slots = corners.shape[0] // counts.shape[0]
    live = (
        (jnp.arange(slots, dtype=jnp.int32)[None, :] < counts[:, None])
        .reshape(-1)
        .astype(jnp.int32)
    )
    before = jnp.cumsum(live, dtype=jnp.int32) - live
    wanted = member * PPD + jnp.arange(PPD, dtype=jnp.int32)
    chosen = ((before[None, :] == wanted[:, None]) & (live[None, :] == 1)).astype(jnp.int32)
    chosen_corner = jnp.sum(chosen[:, :, None] * corners[None, :, :], axis=1, dtype=jnp.int32)
    chosen_level = jnp.sum(chosen * levels[None, :], axis=1, dtype=jnp.int32)
    return (chosen_corner, chosen_level)


def noise_factors(chosen_level):
    sigma_level = 0.5 * jnp.exp(jnp.log(8.0) * chosen_level.astype(jnp.float32) / (NLEV - 1))
    return (sigma_level, lax.rsqrt(1.0 + sigma_level * sigma_level))


def to_tokens(block):
    shaped = block.reshape(PZT, EDGE, PXY, EDGE, PXY, EDGE).transpose(0, 2, 4, 1, 3, 5)
    return shaped.reshape(PZT * PXY * PXY, EDGE * EDGE * EDGE)


def from_tokens(token_rows):
    shaped = token_rows.reshape(PZT, PXY, PXY, EDGE, EDGE, EDGE).transpose(0, 3, 1, 4, 2, 5)
    return shaped.reshape(PZT * EDGE, PXY * EDGE, PXY * EDGE)


def cut_patches(clean, noisy, tangent, z_starts, chosen_corner, chosen_level):
    sigma_level, factor = noise_factors(chosen_level)
    extent = (PZT * EDGE, PXY * EDGE, PXY * EDGE)
    token_list = []
    tangent_list = []
    for number in range(PPD):
        starts = (z_starts[number], chosen_corner[number, 1], chosen_corner[number, 2])
        field = lax.dynamic_slice(clean, starts, extent).astype(jnp.float32)
        field = field + sigma_level[number] * lax.dynamic_slice(noisy, starts, extent).astype(
            jnp.float32
        )
        token_list.append(to_tokens(field * factor[number]).astype(jnp.bfloat16))
        tangent_list.append(to_tokens(lax.dynamic_slice(tangent, starts, extent)))
    return (jnp.stack(token_list), jnp.stack(tangent_list))


def place_scores(buffer, z_starts, chosen_corner, patch_scores):
    extent = (PZT * EDGE, PXY * EDGE, PXY * EDGE)
    for number in range(PPD):
        starts = (z_starts[number], chosen_corner[number, 1], chosen_corner[number, 2])
        block = lax.dynamic_slice(buffer, starts, extent) + from_tokens(patch_scores[number])
        buffer = lax.dynamic_update_slice(buffer, block, starts)
    return buffer


def compute(
    token_rows, chosen_level, tangent_rows, embed, unembed, level_table, pos_embed, w_qkv, w_out
):
    count, tokens_p, voxels = token_rows.shape
    width = embed.shape[1]
    inner = w_out.shape[0]
    heads = inner // HD
    score_scale = 1.0 / HD**0.5
    onehot = (
        chosen_level[:, None] == jnp.arange(level_table.shape[0], dtype=jnp.int32)[None, :]
    ).astype(jnp.bfloat16)
    level_rows = jnp.dot(onehot, level_table, preferred_element_type=jnp.float32)
    hidden0 = jnp.dot(
        token_rows.reshape(count * tokens_p, voxels), embed, preferred_element_type=jnp.float32
    )
    hidden0 = (
        hidden0.reshape(count, tokens_p, width)
        + level_rows[:, None, :]
        + pos_embed.astype(jnp.float32)[None]
    )
    normed_f, unused = layer_normal(hidden0)
    normed = normed_f.astype(jnp.bfloat16).reshape(count * tokens_p, width)
    projected = jnp.dot(normed, w_qkv, preferred_element_type=jnp.float32).reshape(
        count, tokens_p, 3, heads, HD
    )
    query_n, query_r = head_normal(projected[:, :, 0])
    key_n, key_r = head_normal(projected[:, :, 1])
    query_b = query_n.astype(jnp.bfloat16)
    key_b = key_n.astype(jnp.bfloat16)
    value_b = projected[:, :, 2].astype(jnp.bfloat16)
    logits = contract("pqhd,pkhd->phqk", query_b, key_b) * score_scale
    expo = jnp.exp(logits)
    attention_p = expo / jnp.sum(expo, axis=-1, keepdims=True)
    attention_b = attention_p.astype(jnp.bfloat16)
    attended = (
        contract("phqk,pkhd->pqhd", attention_b, value_b)
        .astype(jnp.bfloat16)
        .reshape(count * tokens_p, inner)
    )
    hidden1 = hidden0 + jnp.dot(attended, w_out, preferred_element_type=jnp.float32).reshape(
        count, tokens_p, width
    )
    feat_f, feat_r = layer_normal(hidden1)
    features = feat_f.astype(jnp.bfloat16).reshape(count * tokens_p, width)
    patch_scores = jnp.dot(features, unembed, preferred_element_type=jnp.float32).reshape(
        count, tokens_p, voxels
    )
    d_feat = jnp.dot(
        tangent_rows.reshape(count * tokens_p, voxels),
        unembed.T,
        preferred_element_type=jnp.float32,
    )
    d_feat = d_feat.reshape(count, tokens_p, width)
    d_hidden = feat_r * (
        d_feat
        - jnp.mean(d_feat, axis=-1, keepdims=True)
        - feat_f * jnp.mean(d_feat * feat_f, axis=-1, keepdims=True)
    )
    d_hidden = d_hidden.astype(jnp.bfloat16).reshape(count * tokens_p, width)
    grad_out_term = jnp.dot(attended.T, d_hidden, preferred_element_type=jnp.float32)
    d_att = jnp.dot(d_hidden, w_out.T, preferred_element_type=jnp.float32).astype(jnp.bfloat16)
    d_att = d_att.reshape(count, tokens_p, heads, HD)
    d_probs = contract("pqhd,pkhd->phqk", d_att, value_b)
    d_value = contract("phqk,pqhd->pkhd", attention_b, d_att).astype(jnp.bfloat16)
    row_total = jnp.sum(d_probs * attention_p, axis=-1, keepdims=True)
    d_logits = (attention_p * (d_probs - row_total) * score_scale).astype(jnp.bfloat16)
    d_query_n = contract("phqk,pkhd->pqhd", d_logits, key_b)
    d_key_n = contract("phqk,pqhd->pkhd", d_logits, query_b)
    d_query = (
        query_r * (d_query_n - query_n * jnp.mean(d_query_n * query_n, axis=-1, keepdims=True))
    ).astype(jnp.bfloat16)
    d_key = (key_r * (d_key_n - key_n * jnp.mean(d_key_n * key_n, axis=-1, keepdims=True))).astype(
        jnp.bfloat16
    )
    rows = count * tokens_p
    d_both = jnp.concatenate([d_query.reshape(rows, inner), d_key.reshape(rows, inner)], axis=1)
    grad_qk_term = jnp.dot(normed.T, d_both, preferred_element_type=jnp.float32)
    grad_v_term = jnp.dot(
        normed.T, d_value.reshape(rows, inner), preferred_element_type=jnp.float32
    )
    return (patch_scores, grad_qk_term, grad_v_term, grad_out_term)


def on_device(
    volume,
    noise,
    cotangent,
    patch_corner,
    patch_count,
    patch_level,
    embed,
    unembed,
    level_table,
    pos_embed,
    w_qkv,
    w_out,
):
    planes = volume.shape[0]
    slab_number = lax.axis_index("slab")
    member_number = lax.axis_index("fsdp")
    chosen_corner, chosen_level = pick_patches(
        patch_count[0], patch_corner[0], patch_level[0], member_number
    )
    rim_clean, rim_noise, rim_tangent = from_behind(
        (volume[:HALO], noise[:HALO], cotangent[:HALO]), "slab", -1
    )
    clean = jnp.concatenate([volume, rim_clean], axis=0)
    noisy = jnp.concatenate([noise, rim_noise], axis=0)
    tangent = jnp.concatenate([cotangent, rim_tangent], axis=0)
    local_z = chosen_corner[:, 0] - slab_number * planes
    token_rows, tangent_rows = cut_patches(
        clean, noisy, tangent, local_z, chosen_corner, chosen_level
    )
    full_qkv, full_out = (
        lax.all_gather(w_qkv, "fsdp", axis=0, tiled=True),
        lax.all_gather(w_out, "fsdp", axis=0, tiled=True),
    )
    patch_scores, qk_term, value_term, out_term = compute(
        token_rows,
        chosen_level,
        tangent_rows,
        embed,
        unembed,
        level_table,
        pos_embed,
        full_qkv,
        full_out,
    )
    buffer = place_scores(jnp.zeros(clean.shape, jnp.float32), local_z, chosen_corner, patch_scores)
    summed = lax.psum_scatter(
        buffer.astype(jnp.bfloat16), "fsdp", scatter_dimension=1, tiled=True
    ).astype(jnp.float32)
    arrived = from_behind(summed[planes:].astype(jnp.bfloat16), "slab", 1).astype(jnp.float32)
    score = summed[:planes].at[:HALO].add(arrived)
    qk_part, value_part, out_part = (
        lax.psum_scatter(
            qk_term.astype(jnp.bfloat16), "fsdp", scatter_dimension=0, tiled=True
        ).astype(jnp.float32),
        lax.psum_scatter(
            value_term.astype(jnp.bfloat16), "fsdp", scatter_dimension=0, tiled=True
        ).astype(jnp.float32),
        lax.psum_scatter(
            out_term.astype(jnp.bfloat16), "fsdp", scatter_dimension=0, tiled=True
        ).astype(jnp.float32),
    )
    grad_qk, grad_v, grad_out = (
        lax.psum_scatter(
            qk_part.astype(jnp.bfloat16), "slab", scatter_dimension=1, tiled=True
        ).astype(jnp.float32),
        lax.psum_scatter(
            value_part.astype(jnp.bfloat16), "slab", scatter_dimension=1, tiled=True
        ).astype(jnp.float32),
        lax.psum_scatter(
            out_part.astype(jnp.bfloat16), "slab", scatter_dimension=1, tiled=True
        ).astype(jnp.float32),
    )
    return (score, grad_qk, grad_v, grad_out)


def solution(mesh):
    placed = (
        P("slab", None, None),
        P("slab", None, None),
        P("slab", None, None),
        P("slab", None, None),
        P("slab", None),
        P("slab", None),
        P(),
        P(),
        P(),
        P(),
        P("fsdp", None),
        P("fsdp", None),
    )
    return jax.shard_map(
        on_device,
        mesh=mesh,
        in_specs=placed,
        out_specs=(
            P("slab", "fsdp", None),
            P("fsdp", "slab"),
            P("fsdp", "slab"),
            P("fsdp", "slab"),
        ),
        check_vma=False,
    )
```

profile of v0, /device:TPU:0, one launch (start us, length us, event | category | flops | bytes accessed | tf_op | source)
XLA Modules:
  0.0 524.6 jit_solution(10483747763227846539)
XLA Ops:
  43.7 6.8 %collective-permute-done.1 = bf16[24,128,128]{2,1,0:T(8,128)(2,1)} collective-permute-done((bf16[24,128,128]{2,1,0:T(8,128)(2,1)}, bf16[24,128,128]{2,1,0:T(8,128)(2,1)}, u32[]{:S(2)}, u32[]{:S(2)}) %collective-permute-start.1) | collective-permute-done | bytes 786464 | tf_op jit(solution)/shard_map/ppermute | solution.py:18
  67.1 7.7 %convert_element_type.182 = bf16[1,256,512]{2,1,0:T(8,128)(2,1)} reshape(bf16[4,8,8,8,8,8]{5,4,3,2,1,0:T(8,128)(2,1)} %bitcast.165) | data formatting | bytes 524288 | tf_op jit(solution)/shard_map/convert_element_type | solution.py:77
  84.3 7.7 %convert_element_type.188 = bf16[1,256,512]{2,1,0:T(8,128)(2,1)} reshape(bf16[4,8,8,8,8,8]{5,4,3,2,1,0:T(8,128)(2,1)} %bitcast.166) | data formatting | bytes 524288 | tf_op jit(solution)/shard_map/convert_element_type | solution.py:77
  105.4 7.0 %stack_reshape.6 = bf16[1,256,512]{2,1,0:T(8,128)(2,1)S(1)} reshape(bf16[4,8,8,8,8,8]{5,4,3,2,1,0:T(8,128)(2,1)} %copy.66) | data formatting | bytes 524288 | tf_op jit(solution)/shard_map/stack;reshape | solution.py:79
  121.8 7.9 %stack_reshape.7 = bf16[1,256,512]{2,1,0:T(8,128)(2,1)} reshape(bf16[4,8,8,8,8,8]{5,4,3,2,1,0:T(8,128)(2,1)} %copy.67) | data formatting | bytes 524288 | tf_op jit(solution)/shard_map/stack;reshape | solution.py:79
  137.1 15.9 %copy.59 = bf16[3072,2048]{1,0:T(8,128)(2,1)} copy(bf16[3072,2048]{0,1:T(8,128)(2,1)} %bitcast.169) | data formatting | bytes 25165824 | tf_op jit(solution)/shard_map/dot_general | solution.py:113
  153.0 10.0 %fusion.21 = f32[2,256,3,8,128]{1,4,3,2,0:T(8,128)S(1)} fusion(bf16[3,8,128,2048,1]{3,2,1,0,4:T(8,128)(2,1)} %bitcast.170, bf16[2,256,2048]{2,1,0:T(8,128)(2,1)} %multiply_convert_fusion.2), kind=kOutput, calls=%fused_computation.31 | convolution fusion | flops 6442450944 | bytes 20971520 | tf_op jit(solution)/shard_map/dot_general | solution.py:113
  168.0 8.2 %all-gather.5.cloned.1.call-done = bf16[1024,2048]{1,0:T(8,128)(2,1)} async-done(((bf16[128,2048]{1,0:T(8,128)(2,1)}), bf16[1024,2048]{1,0:T(8,128)(2,1)}) %all-gather.5.cloned.1.call-update) | async-done | bytes 4194320 | tf_op jit(solution)/shard_map/all_gather | solution.py:206
  208.3 6.3 %convolution_convert_fusion.1 = bf16[1024,2048]{1,0:T(8,128)(2,1)} fusion(bf16[512,2048]{1,0:T(8,128)(2,1)} %bitcast.180, bf16[64,8,8,128]{3,2,1,0:T(8,128)(2,1)} %bitcast.183), kind=kOutput, calls=%fused_computation.17 | convolution fusion | flops 2149580800 | bytes 7340032 | tf_op jit(solution)/shard_map/dot_general | solution.py:150
  220.2 10.1 %fusion.13 = f32[2,8,128,256]{3,2,1,0:T(8,128)} fusion(f32[2,8,256,256]{2,3,1,0:T(8,128)} %fusion.53, f32[2,256,3,8,128]{1,4,3,2,0:T(8,128)} %copy-done.2, f32[2,256,8]{1,2,0:T(8,128)S(1)} %add_rsqrt_fusion.1, f32[2,8,256,256]{2,3,1,0:T(8,128)} %copy-done.5, f32[2,8,256]{2,1,0:T(8,128)S(1)} %get-tuple-element.46), kind=kOutput, calls=%fused_computation.23 | convolution fusion | flops 278925568 | bytes 21020672 | tf_op jit(solution)/shard_map/phqk,pqhd->pkhd/dot_general | solution.py:33
  230.3 12.2 %fusion.26 = (f32[2,256,8]{1,2,0:T(8,128)S(1)}, f32[2,256,8]{1,2,0:T(8,128)S(1)}, f32[2,8,128,256]{3,2,1,0:T(8,128)}) fusion(f32[2,256,3,8,128]{1,4,3,2,0:T(8,128)} %copy-done.2, f32[2,256,8]{1,2,0:T(8,128)S(1)} %add_rsqrt_fusion.1, f32[2,256,8]{1,2,0:T(8,128)S(1)} %add_rsqrt_fusion, f32[2,8,128,256]{3,2,1,0:T(8,128)} %fusion.13, ...), kind=kOutput, calls=%fused_computation.40 | convolution fusion | flops 282063104 | bytes 27377664 | tf_op jit(solution)/shard_map/phqk,pkhd->pqhd/dot_general | solution.py:33
  256.5 9.7 %convolution_convert_fusion = bf16[2048,2048]{1,0:T(8,128)(2,1)} fusion(bf16[512,2048]{1,0:T(8,128)(2,1)} %bitcast.177, bf16[512,1024]{1,0:T(8,128)(2,1)} %bitcast.181, bf16[512,1024]{1,0:T(8,128)(2,1)S(1)} %bitcast.182), kind=kOutput, calls=%fused_computation.1 | convolution fusion | flops 4303355904 | bytes 12582912 | tf_op jit(solution)/shard_map/dot_general | solution.py:167
  270.0 6.4 %reshape_squeeze.6 = f32[4,8,8,8,8,8]{5,4,3,2,1,0:T(8,128)} reshape(f32[256,512]{1,0:T(8,128)S(1)} %get-tuple-element.31) | data formatting | bytes 1048576 | tf_op jit(solution)/shard_map/reshape;squeeze | solution.py:62
  276.4 11.5 %copy.64 = f32[4,8,8,8,8,8]{5,4,3,2,1,0:T(8,128)} copy(f32[4,8,8,8,8,8]{5,3,1,4,2,0:T(8,128)} %bitcast.163) | data formatting | bytes 1048576 | tf_op jit(solution)/shard_map/transpose | solution.py:62
  293.5 7.3 %reshape_squeeze.7 = f32[4,8,8,8,8,8]{5,4,3,2,1,0:T(8,128)} reshape(f32[256,512]{1,0:T(8,128)} %get-tuple-element.30) | data formatting | bytes 1048576 | tf_op jit(solution)/shard_map/reshape;squeeze | solution.py:62
  300.9 11.8 %copy.65 = f32[4,8,8,8,8,8]{5,4,3,2,1,0:T(8,128)} copy(f32[4,8,8,8,8,8]{5,3,1,4,2,0:T(8,128)} %bitcast.164) | data formatting | bytes 1048576 | tf_op jit(solution)/shard_map/transpose | solution.py:62
  312.7 6.6 %reshape.313 = f32[32,64,64]{2,1,0:T(8,128)} reshape(f32[4,8,8,8,8,8]{5,4,3,2,1,0:T(8,128)} %copy.65) | data formatting | bytes 1048576 | tf_op jit(solution)/shard_map/reshape | solution.py:63
  321.5 10.3 %dynamic_update_slice.6 = f32[56,128,128]{2,1,0:T(8,128)} dynamic-update-slice(f32[56,128,128]{2,1,0:T(8,128)} %broadcast_in_dim.2, f32[32,64,64]{2,1,0:T(8,128)S(1)} %reshape.312, s32[]{:T(128)S(6)} %select_n.12, s32[]{:T(128)S(6)} %select_n.13, s32[]{:T(128)S(6)} %select_n.14) | dynamic-update-slice | bytes 1048580 | tf_op jit(solution)/shard_map/dynamic_update_slice | solution.py:87
  333.8 15.8 %dynamic_update_slice.7 = f32[56,128,128]{2,1,0:T(8,128)} dynamic-update-slice(f32[56,128,128]{2,1,0:T(8,128)} %dynamic_update_slice.6, f32[32,64,64]{2,1,0:T(8,128)S(1)} %dynamic-slice_add_fusion, s32[]{:T(128)S(6)} %select_n.15, s32[]{:T(128)S(6)} %select_n.16, s32[]{:T(128)S(6)} %select_n.17) | dynamic-update-slice | bytes 1048580 | tf_op jit(solution)/shard_map/dynamic_update_slice | solution.py:87
  354.9 41.0 %reduce-scatter.10.cloned.1.call-done = bf16[256,2048]{1,0:T(8,128)(2,1)} async-done(((bf16[2048,2048]{1,0:T(8,128)(2,1)}), bf16[256,2048]{1,0:T(8,128)(2,1)}) %reduce-scatter.10.cloned.1.call-update) | async-done | bytes 1048592 | tf_op jit(solution)/shard_map/reduce_scatter | solution.py:226
  395.9 35.7 %reduce-scatter.8.cloned.1.call-done = bf16[56,16,128]{2,1,0:T(8,128)(2,1)} async-done(((bf16[56,128,128]{2,1,0:T(8,128)(2,1)}), bf16[56,16,128]{2,1,0:T(8,128)(2,1)}) %reduce-scatter.8.cloned.1.call-update) | async-done | bytes 229392 | tf_op jit(solution)/shard_map/reduce_scatter | solution.py:220
  438.2 19.2 %reduce-scatter.16.cloned.1.call-done = bf16[256,256]{1,0:T(8,128)(2,1)} async-done(((bf16[256,1024]{1,0:T(8,128)(2,1)}), bf16[256,256]{1,0:T(8,128)(2,1)}) %reduce-scatter.16.cloned.1.call-update) | async-done | bytes 131088 | tf_op jit(solution)/shard_map/reduce_scatter | solution.py:240
  459.1 26.2 %reduce-scatter.20.cloned.1.call-done = bf16[128,512]{1,0:T(8,128)(2,1)} async-done(((bf16[128,2048]{1,0:T(8,128)(2,1)}), bf16[128,512]{1,0:T(8,128)(2,1)}) %reduce-scatter.20.cloned.1.call-update) | async-done | bytes 131088 | tf_op jit(solution)/shard_map/reduce_scatter | solution.py:243
  486.9 29.0 %reduce-scatter.12.cloned.1.call-done = bf16[256,512]{1,0:T(8,128)(2,1)} async-done(((bf16[256,2048]{1,0:T(8,128)(2,1)}), bf16[256,512]{1,0:T(8,128)(2,1)}) %reduce-scatter.12.cloned.1.call-update) | async-done | bytes 262160 | tf_op jit(solution)/shard_map/reduce_scatter | solution.py:237
  (148 shorter events, 168.6 us)
Async XLA Ops:
  7.2 175.5 %copy-start = (bf16[2048,512]{1,0:T(8,128)(2,1)S(1)}, bf16[2048,512]{1,0:T(8,128)(2,1)}, u32[]{:S(2)}) copy-start(bf16[2048,512]{1,0:T(8,128)(2,1)} %param.21) | copy-start | bytes 6291460
  7.2 11.5 %copy-start.6 = (bf16[32,128,128]{2,1,0:T(8,128)(2,1)S(1)}, bf16[32,128,128]{2,1,0:T(8,128)(2,1)}, u32[]{:S(2)}) copy-start(bf16[32,128,128]{2,1,0:T(8,128)(2,1)} %param.14) | copy-start | bytes 3145732
  7.2 11.2 %copy-start.16 = (s32[1,8]{1,0:T(1,128)S(1)}, s32[1,8]{1,0:T(1,128)}, u32[]{:S(2)}) copy-start(s32[1,8]{1,0:T(1,128)} %param.18) | copy-start | bytes 100
  7.2 129.9 %all-gather.3.cloned.1.call-start = ((), (), s32[]{:S(2)}) async-start(), calls=%async_computation.7 | async-start | bytes 14155776 | tf_op jit(solution)/shard_map/all_gather | solution.py:205
  7.9 168.2 %all-gather.5.cloned.1.call-start = ((), (), s32[]{:S(2)}) async-start(), calls=%async_computation.8 | async-start | bytes 4718592 | tf_op jit(solution)/shard_map/all_gather | solution.py:206
  10.1 31.4 %collective-permute-start = (bf16[24,128,128]{2,1,0:T(8,128)(2,1)}, bf16[24,128,128]{2,1,0:T(8,128)(2,1)}, u32[]{:S(2)}, u32[]{:S(2)}) collective-permute-start(bf16[24,128,128]{2,1,0:T(8,128)(2,1)} %slice.100), channel_id=1, source_target_pairs={{8,0},{16,8},{24,16},{9,1},{17,9},{25,17},{10,2},{18,10},{26,18},{... | collective-permute-start | bytes 2359304 | tf_op jit(solution)/shard_map/ppermute | solution.py:18
  13.5 10.1 %copy-start.15 = (s32[1,32,3]{1,0,2:T(1,128)S(1)}, s32[1,32,3]{1,0,2:T(1,128)}, u32[]{:S(2)}) copy-start(s32[1,32,3]{1,0,2:T(1,128)} %param.17) | copy-start | bytes 1156
  13.5 10.1 %copy-start.17 = (s32[1,32]{1,0:T(1,128)S(1)}, s32[1,32]{1,0:T(1,128)}, u32[]{:S(2)}) copy-start(s32[1,32]{1,0:T(1,128)} %param.19) | copy-start | bytes 388
  13.5 37.0 %collective-permute-start.1 = (bf16[24,128,128]{2,1,0:T(8,128)(2,1)}, bf16[24,128,128]{2,1,0:T(8,128)(2,1)}, u32[]{:S(2)}, u32[]{:S(2)}) collective-permute-start(bf16[24,128,128]{2,1,0:T(8,128)(2,1)} %slice.106), channel_id=1, source_target_pairs={{8,0},{16,8},{24,16},{9,1},{17,9},{25,17},{10,2},{18,10},{26,18},{... | collective-permute-start | bytes 2359304 | tf_op jit(solution)/shard_map/ppermute | solution.py:18
  17.0 74.9 %collective-permute-start.3 = (bf16[24,128,128]{2,1,0:T(8,128)(2,1)}, bf16[24,128,128]{2,1,0:T(8,128)(2,1)}, u32[]{:S(2)}, u32[]{:S(2)}) collective-permute-start(bf16[24,128,128]{2,1,0:T(8,128)(2,1)} %slice.121), channel_id=1, source_target_pairs={{8,0},{16,8},{24,16},{9,1},{17,9},{25,17},{10,2},{18,10},{26,18},{... | collective-permute-start | bytes 2359304 | tf_op jit(solution)/shard_map/ppermute | solution.py:18
  18.4 335.1 %reduce-scatter.14.cloned.1.call-start = ((), (), s32[]{:S(2)}) async-start(), calls=%async_computation.12 | async-start | bytes 4718592 | tf_op jit(solution)/shard_map/reduce_scatter | solution.py:229
  18.6 3.7 copy-start.7
  19.7 13.6 %copy-start.10 = (bf16[256,2048]{1,0:T(8,128)(2,1)S(1)}, bf16[256,2048]{1,0:T(8,128)(2,1)}, u32[]{:S(2)}) copy-start(bf16[256,2048]{1,0:T(8,128)(2,1)} %param.23) | copy-start | bytes 3145732
  38.5 12.0 %copy-start.8 = (bf16[56,128,128]{2,1,0:T(8,128)(2,1)S(1)}, bf16[56,128,128]{2,1,0:T(8,128)(2,1)}, u32[]{:S(2)}) copy-start(bf16[56,128,128]{2,1,0:T(8,128)(2,1)} %constant_dynamic-update-slice_fusion.3) | copy-start | bytes 5505028
  121.8 7.9 %copy-start.12 = (bf16[1,256,512]{2,1,0:T(8,128)(2,1)S(1)}, bf16[1,256,512]{2,1,0:T(8,128)(2,1)}, u32[]{:S(2)}) copy-start(bf16[1,256,512]{2,1,0:T(8,128)(2,1)} %convert_element_type.182) | copy-start | bytes 786436
  121.8 7.9 %copy-start.13 = (bf16[1,256,512]{2,1,0:T(8,128)(2,1)S(1)}, bf16[1,256,512]{2,1,0:T(8,128)(2,1)}, u32[]{:S(2)}) copy-start(bf16[1,256,512]{2,1,0:T(8,128)(2,1)} %convert_element_type.188) | copy-start | bytes 786436
  206.8 147.4 %reduce-scatter.18.cloned.1.call-start = ((), (), s32[]{:S(2)}) async-start(), calls=%async_computation.14 | async-start | bytes 4718592 | tf_op jit(solution)/shard_map/reduce_scatter | solution.py:232
  214.6 181.4 %reduce-scatter.10.cloned.1.call-start = ((), (), s32[]{:S(2)}) async-start(), calls=%async_computation.10 | async-start | bytes 9437184 | tf_op jit(solution)/shard_map/reduce_scatter | solution.py:226
  266.2 165.4 %reduce-scatter.8.cloned.1.call-start = ((), (), s32[]{:S(2)}) async-start(), calls=%async_computation.9 | async-start | bytes 2064384 | tf_op jit(solution)/shard_map/reduce_scatter | solution.py:220
  353.4 104.1 %reduce-scatter.16.cloned.1.call-start = ((), (), s32[]{:S(2)}) async-start(), calls=%async_computation.13 | async-start | bytes 655360 | tf_op jit(solution)/shard_map/reduce_scatter | solution.py:240
  354.1 131.2 %reduce-scatter.20.cloned.1.call-start = ((), (), s32[]{:S(2)}) async-start(), calls=%async_computation.15 | async-start | bytes 655360 | tf_op jit(solution)/shard_map/reduce_scatter | solution.py:243
  354.9 161.1 %reduce-scatter.12.cloned.1.call-start = ((), (), s32[]{:S(2)}) async-start(), calls=%async_computation.11 | async-start | bytes 1310720 | tf_op jit(solution)/shard_map/reduce_scatter | solution.py:237
  432.5 5.7 %collective-permute-start.2 = (bf16[24,16,128]{2,1,0:T(8,128)(2,1)S(1)}, bf16[24,16,128]{2,1,0:T(8,128)(2,1)S(1)}, u32[]{:S(2)}, u32[]{:S(2)}) collective-permute-start(bf16[24,16,128]{2,1,0:T(8,128)(2,1)S(1)} %slice.129), channel_id=1, source_target_pairs={{0,8},{8,16},{16,24},{1,9},{9,17},{17,25},{2,10},{10,18},{18,26},{... | collective-permute-start | bytes 294920 | tf_op jit(solution)/shard_map/ppermute | solution.py:18
  438.2 79.5 %copy-start.14 = (f32[32,16,128]{2,1,0:T(8,128)}, f32[32,16,128]{2,1,0:T(8,128)S(1)}, u32[]{:S(2)}) copy-start(f32[32,16,128]{2,1,0:T(8,128)S(1)} %fusion.61) | copy-start | bytes 786436
  (7 other events, 14.9 us)
Sparse Core Ops, SparseCore 0:
  9.7 119.4 all-gather.2
  130.7 45.3 all-gather.4
  206.9 48.7 reduce-scatter.13
  257.8 48.1 reduce-scatter.17
  308.1 87.7 reduce-scatter.9
  398.1 33.4 reduce-scatter.7
  434.5 22.9 reduce-scatter.15
  460.5 24.7 reduce-scatter.19
  488.2 27.6 reduce-scatter.11
where the time goes:
time: 531 us; the launch traced here: 525 us
  local copies, waits for them, and re-layouts  206 us (39%)
  waiting for transfers between devices  169 us (32%)
  matrix products  84.7 us (16%)
  other arithmetic  31.3 us (6%)
  between operations  25.5 us (5%)
  starting transfers between devices  7.96 us (1%)
    reduce_scatter x1, waiting for transfers between devices, on_device(): lax.psum_scatter(qk_term.astype(jnp.bfloat16), 'fsdp', scatter_dimension=...  41 us
    reduce_scatter x1, waiting for transfers between devices, on_device(): lax.psum_scatter(buffer.astype(jnp.bfloat16), 'fsdp', scatter_dimension=1...  35.7 us
    convert_element_type x6, local copies, waits for them, and re-layouts, cut_patches(): token_list.append(to_tokens(field * factor[number]).astype(jnp.bfloat16))  34.5 us
    dot_general x6, matrix products, contract(): return jnp.einsum(form, left, right, preferred_element_type=jnp.float32)  33.2 us
    reduce_scatter x1, waiting for transfers between devices, on_device(): lax.psum_scatter(qk_part.astype(jnp.bfloat16), 'slab', scatter_dimension=...  29 us
    reduce_scatter x1, waiting for transfers between devices, on_device(): lax.psum_scatter(out_part.astype(jnp.bfloat16), 'slab', scatter_dimension...  26.2 us
    dynamic_update_slice x2, local copies, waits for them, and re-layouts, place_scores(): buffer = lax.dynamic_update_slice(buffer, block, starts)  26.1 us
    transpose x2, local copies, waits for them, and re-layouts, from_tokens(): token_rows.reshape(PZT, PXY, PXY, EDGE, EDGE, EDGE)  23.3 us
  transfers between devices with their start and end apart: 13, of which 8 were waited for; matrix products, arithmetic and copies ran while one was open for 54% of the time, Pallas kernels for 0%

commit v1 on v0

v1 whole, which is shorter than its diff:
```python
import functools

import jax
import jax.numpy as jnp
from jax import lax
from jax.experimental import pallas as pl
from jax.experimental.pallas import tpu as pltpu
from jax.sharding import PartitionSpec as P

HD = 128
NLEV = 1000
EDGE = 8
PXY = 8
PZT = 4
PPD = 2
HALO = 24
TOK = PZT * PXY * PXY
VOX = EDGE * EDGE * EDGE
KINDS = 3
LANES = 128

F32 = jnp.float32
BF16 = jnp.bfloat16
VMEM = pltpu.MemorySpace.VMEM
SMEM = pltpu.MemorySpace.SMEM
PARAMS = pltpu.CompilerParams(vmem_limit_bytes=48 * 1024 * 1024)


def swap(block, axis, pairs):
    return lax.ppermute(block, axis, pairs)


def across(block, axis, size, k):
    return lax.ppermute(block, axis, [(i, i ^ k) for i in range(size)])


def rows_dot(left, right):
    return lax.dot_general(left, right, (((1,), (0,)), ((), ())), preferred_element_type=F32)


def last_dot(left, right):
    return lax.dot_general(left, right, (((1,), (1,)), ((), ())), preferred_element_type=F32)


def first_dot(left, right):
    return lax.dot_general(left, right, (((0,), (0,)), ((), ())), preferred_element_type=F32)


def pick_patches(counts, corners, levels, first, number):
    slots = corners.shape[0] // counts.shape[0]
    live = (
        (jnp.arange(slots, dtype=jnp.int32)[None, :] < counts[:, None])
        .reshape(-1)
        .astype(jnp.int32)
    )
    before = jnp.cumsum(live, dtype=jnp.int32) - live
    wanted = first + jnp.arange(number, dtype=jnp.int32)
    chosen = ((before[None, :] == wanted[:, None]) & (live[None, :] == 1)).astype(jnp.int32)
    chosen_corner = jnp.sum(chosen[:, :, None] * corners[None, :, :], axis=1, dtype=jnp.int32)
    chosen_level = jnp.sum(chosen * levels[None, :], axis=1, dtype=jnp.int32)
    return (chosen_corner, chosen_level)


def noise_factors(chosen_level):
    sigma_level = 0.5 * jnp.exp(jnp.log(8.0) * chosen_level.astype(F32) / (NLEV - 1))
    return (sigma_level, lax.rsqrt(1.0 + sigma_level * sigma_level))


def exchange_groups(tiles, lane):
    for bit in range(3):
        step = 1 << bit
        upper = ((lane >> (3 + bit)) & 1) == 1
        fresh = []
        for i in range(8):
            other = tiles[i ^ step]
            if i & step:
                moved = pltpu.roll(other, LANES - 8 * step, 1)
                fresh.append(jnp.where(upper, tiles[i], moved))
            else:
                moved = pltpu.roll(other, 8 * step, 1)
                fresh.append(jnp.where(upper, moved, tiles[i]))
        tiles = fresh
    return tiles


def cut_kernel(noisy, corner_ref, factor_ref, *refs):
    if noisy:
        field_ref, noise_ref, out_ref, work = refs
    else:
        field_ref, out_ref, work = refs
    number = pl.program_id(0)
    z0 = corner_ref[number, 0]
    y0 = corner_ref[number, 1]
    x0 = corner_ref[number, 2]
    lane = lax.broadcasted_iota(jnp.int32, (8, LANES), 1)
    low = lax.broadcasted_iota(jnp.int32, (64, LANES), 1) < 64
    for pair in range(PZT // 2):
        for ez in range(0, EDGE, 2):
            halves = []
            for half in range(2):
                z = z0 + (2 * pair + half) * EDGE + ez
                planes = []
                for odd in range(2):
                    plane = field_ref[z + odd, pl.ds(y0, PXY)].astype(F32)
                    if noisy:
                        noise = noise_ref[z + odd, pl.ds(y0, PXY)].astype(F32)
                        plane = (plane + factor_ref[number, 0] * noise) * factor_ref[number, 1]
                    plane = plane.reshape(64, LANES)
                    shift = lax.rem(LANES + 64 * odd - x0, LANES)
                    planes.append(pltpu.roll(plane, shift, 1))
                work[half] = jnp.where(low, planes[0], planes[1])
                tiles = [work[half, pl.ds(ey, 8, stride=8), :] for ey in range(8)]
                halves.append(exchange_groups(tiles, lane))
            for px in range(PXY):
                row = px * 32 + pair * 16
                both = jnp.concatenate([halves[0][px], halves[1][px]], axis=0)
                out_ref[0, row : row + 16, (ez // 2) * LANES : (ez // 2 + 1) * LANES] = both.astype(
                    BF16
                )


def cut_tokens(corner, factors, fields):
    count = corner.shape[0]
    shaped = [f.reshape(f.shape[0], f.shape[1] // 8, 8, LANES) for f in fields]
    whole = [pl.BlockSpec(f.shape, lambda i: (0, 0, 0, 0)) for f in shaped]
    return pl.pallas_call(
        functools.partial(cut_kernel, len(fields) == 2),
        grid=(count,),
        in_specs=[pl.BlockSpec(memory_space=SMEM)] * 2 + whole,
        out_specs=pl.BlockSpec((1, TOK, VOX), lambda i: (i, 0, 0)),
        out_shape=jax.ShapeDtypeStruct((count, TOK, VOX), BF16),
        scratch_shapes=[pltpu.VMEM((2, 64, LANES), F32)],
        compiler_params=PARAMS,
        name="cut_tokens",
    )(corner, factors, *shaped)


def place_kernel(corner_ref, *refs):
    score_refs = refs[:PPD]
    out_ref, buffer, work = refs[PPD:]
    lane = lax.broadcasted_iota(jnp.int32, (8, LANES), 1)
    wide = lax.broadcasted_iota(jnp.int32, (64, LANES), 1)
    buffer[...] = jnp.zeros_like(buffer)
    for number in range(PPD):
        z0 = corner_ref[number, 0]
        y0 = corner_ref[number, 1]
        x0 = corner_ref[number, 2]
        inside = (wide >= x0) & (wide < x0 + 64)
        for pz in range(PZT):
            for ez in range(0, EDGE, 2):
                tiles = [
                    score_refs[number][
                        px * 32 + pz * 8 : px * 32 + pz * 8 + 8,
                        (ez // 2) * LANES : (ez // 2 + 1) * LANES,
                    ].astype(F32)
                    for px in range(PXY)
                ]
                tiles = exchange_groups(tiles, lane)
                slot = (ez // 2) % 2
                for ey in range(8):
                    work[slot, pl.ds(ey, 8, stride=8), :] = tiles[ey]
                both = work[slot]
                for odd in range(2):
                    plane = pltpu.roll(both, lax.rem(LANES + x0 - 64 * odd, LANES), 1)
                    plane = jnp.where(inside, plane, 0.0).reshape(PXY, 8, LANES)
                    z = z0 + pz * EDGE + ez + odd
                    buffer[z, pl.ds(y0, PXY)] += plane
    out_ref[...] = buffer[...].astype(BF16)


def place_scores(corner, scores, planes, rows):
    shape = (planes, rows // 8, 8, LANES)
    out = pl.pallas_call(
        place_kernel,
        in_specs=[pl.BlockSpec(memory_space=SMEM)] + [pl.BlockSpec(memory_space=VMEM)] * PPD,
        out_specs=pl.BlockSpec(memory_space=VMEM),
        out_shape=jax.ShapeDtypeStruct(shape, BF16),
        scratch_shapes=[pltpu.VMEM(shape, F32), pltpu.VMEM((2, 64, LANES), F32)],
        compiler_params=PARAMS,
        name="place_scores",
    )(corner, *scores)
    return out.reshape(planes, rows, LANES)


def fold_kernel(members, me_ref, embed_ref, pos_ref, level_ref, *refs):
    w_refs, out_ref = refs[:members], refs[members]
    me = me_ref[0]
    width = embed_ref.shape[1]
    depth = w_refs[0].shape[0]
    start = 0
    column = jnp.zeros((1, HD), F32)
    for k in range(members):
        column += jnp.sum(w_refs[k][...].astype(F32), axis=0, keepdims=True)
    for part in (embed_ref, pos_ref, level_ref):
        rows = part.shape[0]
        total = jnp.zeros((rows, HD), F32)
        for k in range(members):
            at = pl.multiple_of(jnp.bitwise_xor(me, k) * depth, LANES)
            total += rows_dot(part[:, pl.ds(at, depth)], w_refs[k][...])
        mean = jnp.sum(part[...].astype(F32), axis=1, keepdims=True) / width
        out_ref[start : start + rows, :] = (total - mean * column).astype(BF16)
        start += rows


def fold_weights(me, embed, pos, level, blocks):
    rows = embed.shape[0] + pos.shape[0] + level.shape[0]
    return pl.pallas_call(
        functools.partial(fold_kernel, len(blocks)),
        in_specs=[pl.BlockSpec(memory_space=SMEM)]
        + [pl.BlockSpec(memory_space=VMEM)] * (3 + len(blocks)),
        out_specs=pl.BlockSpec(memory_space=VMEM),
        out_shape=jax.ShapeDtypeStruct((rows, HD), BF16),
        compiler_params=PARAMS,
        name="fold_weights",
    )(me, embed, pos, level, *blocks)


def head_normal(values):
    inverse = lax.rsqrt(jnp.mean(values * values, axis=-1, keepdims=True) + 1e-06)
    return (values * inverse, inverse)


def attention(info_ref, token_ref, scale_ref, fold_refs):
    tokens = token_ref[0]
    rows = fold_refs[0].shape[1]
    patches = rows - VOX - TOK
    where_level = info_ref[1] + jnp.bitwise_xor(info_ref[0], pl.program_id(0)) * PPD
    onehot = (lax.broadcasted_iota(jnp.int32, (TOK, patches), 1) == where_level).astype(BF16)
    scale = jnp.transpose(jnp.broadcast_to(scale_ref[0], (HD, TOK)))
    kinds = []
    for ref in fold_refs:
        total = rows_dot(tokens, ref[0, :VOX])
        total += ref[0, VOX : VOX + TOK].astype(F32)
        total += rows_dot(onehot, ref[0, VOX + TOK :])
        kinds.append(total * scale)
    query_n, query_r = head_normal(kinds[0])
    key_n, key_r = head_normal(kinds[1])
    query_b, key_b, value_b = (query_n.astype(BF16), key_n.astype(BF16), kinds[2].astype(BF16))
    expo = jnp.exp(last_dot(query_b, key_b) * (1.0 / HD**0.5))
    probs = expo / jnp.sum(expo, axis=-1, keepdims=True)
    return (
        tokens,
        onehot,
        scale,
        (query_n, query_r, query_b),
        (key_n, key_r, key_b),
        value_b,
        probs,
        probs.astype(BF16),
    )


def forward_kernel(info_ref, token_ref, scale_ref, q_ref, k_ref, v_ref, out_ref):
    state = attention(info_ref, token_ref, scale_ref, (q_ref, k_ref, v_ref))
    out_ref[0] = rows_dot(state[7], state[5]).astype(BF16)


def backward_kernel(info_ref, token_ref, scale_ref, q_ref, k_ref, v_ref, d_ref, last_ref, out_ref):
    step = pl.program_id(0)
    tokens, onehot, scale, query, key, value_b, probs, probs_b = attention(
        info_ref, token_ref, scale_ref, (q_ref, k_ref, v_ref)
    )
    query_n, query_r, query_b = query
    key_n, key_r, key_b = key
    d_att = d_ref[0]
    d_probs = last_dot(d_att, value_b)
    d_value = first_dot(probs_b, d_att)
    row_total = jnp.sum(d_probs * probs, axis=-1, keepdims=True)
    d_logits = (probs * (d_probs - row_total) * (1.0 / HD**0.5)).astype(BF16)
    d_query_n = rows_dot(d_logits, key_b)
    d_key_n = first_dot(d_logits, query_b)
    d_query = query_r * (
        d_query_n - query_n * jnp.mean(d_query_n * query_n, axis=-1, keepdims=True)
    )
    d_key = key_r * (d_key_n - key_n * jnp.mean(d_key_n * key_n, axis=-1, keepdims=True))

    @pl.when(step == 0)
    def _():
        out_ref[...] = last_ref[...]

    for kind, grad in enumerate((d_query, d_key, d_value)):
        grad = (grad * scale).astype(BF16)
        out_ref[kind, :VOX] += first_dot(tokens, grad)
        out_ref[kind, VOX : VOX + TOK] += grad.astype(F32)
        out_ref[kind, VOX + TOK :] += first_dot(onehot, grad)


def attention_specs(number, heads, rows):
    def at_patch(k, info):
        return (jnp.bitwise_xor(info[0], k) * PPD + number, 0, 0)

    def kind_spec(kind):
        return pl.BlockSpec((1, rows, HD), lambda k, info: (info[2 + kind], 0, 0))

    return [
        pl.BlockSpec((1, TOK, VOX), at_patch),
        pl.BlockSpec((1, 1, TOK), lambda k, info: (k, 0, 0)),
    ] + [kind_spec(kind) for kind in range(KINDS)]


def forward_heads(number, info, tokens, scale, folds):
    heads = scale.shape[0]
    rows = folds.shape[1]
    return pl.pallas_call(
        forward_kernel,
        grid_spec=pltpu.PrefetchScalarGridSpec(
            num_scalar_prefetch=1,
            grid=(heads,),
            in_specs=attention_specs(number, heads, rows),
            out_specs=pl.BlockSpec((1, TOK, HD), lambda k, info: (k, 0, 0)),
        ),
        out_shape=jax.ShapeDtypeStruct((heads, TOK, HD), BF16),
        compiler_params=PARAMS,
        name="forward_heads",
    )(info, tokens, scale, folds, folds, folds)


def backward_heads(number, info, tokens, scale, folds, d_att, last):
    heads = scale.shape[0]
    rows = folds.shape[1]
    whole = pl.BlockSpec((KINDS, rows, HD), lambda k, info: (0, 0, 0))
    return pl.pallas_call(
        backward_kernel,
        grid_spec=pltpu.PrefetchScalarGridSpec(
            num_scalar_prefetch=1,
            grid=(heads,),
            in_specs=attention_specs(number, heads, rows)
            + [pl.BlockSpec((1, TOK, HD), lambda k, info: (k, 0, 0)), whole],
            out_specs=whole,
        ),
        out_shape=jax.ShapeDtypeStruct((KINDS, rows, HD), F32),
        compiler_params=PARAMS,
        name="backward_heads",
    )(info, tokens, scale, folds, folds, folds, d_att, last)


def output_kernel(heads, me_ref, hidden_ref, cot_ref, w_ref, unembed_ref, *refs):
    att_refs = refs[:heads]
    score_ref, wide_ref, d_hidden_ref, d_att_ref, work = refs[heads:]
    me = me_ref[0]
    for k in range(heads):
        at = pl.multiple_of(jnp.bitwise_xor(me, k) * HD, HD)
        wide_ref[:, pl.ds(at, HD)] = att_refs[k][...]
    hidden = hidden_ref[...] + rows_dot(wide_ref[...], w_ref[...])
    centre = hidden - jnp.mean(hidden, axis=-1, keepdims=True)
    inverse = lax.rsqrt(jnp.mean(centre * centre, axis=-1, keepdims=True) + 1e-05)
    feat = centre * inverse
    score_ref[...] = rows_dot(feat.astype(BF16), unembed_ref[...])
    d_feat = last_dot(cot_ref[...], unembed_ref[...])
    d_hidden = inverse * (
        d_feat
        - jnp.mean(d_feat, axis=-1, keepdims=True)
        - feat * jnp.mean(d_feat * feat, axis=-1, keepdims=True)
    )
    d_hidden = d_hidden.astype(BF16)
    d_hidden_ref[...] = d_hidden
    work[...] = last_dot(d_hidden, w_ref[...]).astype(BF16)
    for k in range(heads):
        at = pl.multiple_of(jnp.bitwise_xor(me, k) * HD, HD)
        d_att_ref[k] = work[:, pl.ds(at, HD)]


def output_part(me, hidden, cot, w_out, unembed, attended):
    heads = len(attended)
    inner, width = w_out.shape
    shape = jax.ShapeDtypeStruct
    return pl.pallas_call(
        functools.partial(output_kernel, heads),
        in_specs=[pl.BlockSpec(memory_space=SMEM)]
        + [pl.BlockSpec(memory_space=VMEM)] * (4 + heads),
        out_specs=[pl.BlockSpec(memory_space=VMEM)] * 4,
        out_shape=[
            shape((TOK, VOX), F32),
            shape((TOK, inner), BF16),
            shape((TOK, width), BF16),
            shape((heads, TOK, HD), BF16),
        ],
        scratch_shapes=[pltpu.VMEM((TOK, inner), BF16)],
        compiler_params=PARAMS,
        name="output_part",
    )(me, hidden, cot, w_out, unembed, *attended)


def expand_kernel(heads, blocks, me_ref, embed_ref, pos_ref, level_ref, own_ref, *refs):
    in_refs, (out_ref, work) = refs[:-2], refs[-2:]
    total = own_ref[...].astype(F32)
    for ref in in_refs:
        total += ref[...].astype(F32)
    total = total.astype(BF16)
    split = embed_ref.shape[0]
    after = split + pos_ref.shape[0]
    grad = first_dot(embed_ref[...], total[:split])
    grad += first_dot(pos_ref[...], total[split:after])
    grad += first_dot(level_ref[...], total[after:])
    grad -= jnp.mean(grad, axis=0, keepdims=True)
    work[...] = grad.astype(BF16)
    depth = out_ref.shape[1]
    base = (me_ref[0] // heads) * heads
    for k in range(heads):
        member = base + jnp.bitwise_xor(lax.rem(me_ref[0], heads), k)
        out_ref[k] = work[pl.ds(pl.multiple_of(member * depth, depth), depth), :]


def expand_sums(me, heads, depth, embed, pos, level, own, others):
    width = embed.shape[1]
    columns = own.shape[1]
    return pl.pallas_call(
        functools.partial(expand_kernel, heads, len(others)),
        in_specs=[pl.BlockSpec(memory_space=SMEM)]
        + [pl.BlockSpec(memory_space=VMEM)] * (4 + len(others)),
        out_specs=pl.BlockSpec(memory_space=VMEM),
        out_shape=jax.ShapeDtypeStruct((heads, depth, columns), BF16),
        scratch_shapes=[pltpu.VMEM((width, columns), BF16)],
        compiler_params=PARAMS,
        name="expand_sums",
    )(me, embed, pos, level, own, *others)


def on_device(
    slabs,
    members,
    volume,
    noise,
    cotangent,
    patch_corner,
    patch_count,
    patch_level,
    embed,
    unembed,
    level_table,
    pos_embed,
    w_qkv,
    w_out,
):
    planes, side = volume.shape[:2]
    width = embed.shape[1]
    inner = w_out.shape[0] * members
    heads = inner // HD
    groups = members // heads
    depth = w_qkv.shape[0]
    slab = lax.axis_index("slab")
    member = lax.axis_index("fsdp")
    group, head = member // heads, member % heads
    core = member % 2

    def in_group(block, k):
        pairs = [(i, (i // heads) * heads + ((i % heads) ^ k)) for i in range(members)]
        return swap(block, "fsdp", pairs)

    def among_slabs(block, k):
        return across(block, "slab", slabs, k)

    me = jnp.reshape(member, (1,)).astype(jnp.int32)

    kind = slab % KINDS
    w_blocks = []
    for k in range(members):
        to = (member ^ k) % heads
        block = lax.dynamic_slice(w_qkv, (0, kind * inner + to * HD), (depth, HD))
        w_blocks.append(across(block, "fsdp", members, k) if k else block)

    part = HALO // 2
    rims = jnp.stack(
        [
            lax.dynamic_slice(f, (core * part, 0, 0), (part, side, side))
            for f in (volume, noise, cotangent)
        ]
    )
    rims = swap(rims, "slab", [(i, i - 1) for i in range(1, slabs)])
    other = across(rims, "fsdp", members, 1)
    first = jnp.where(core == 0, rims, other)
    second = jnp.where(core == 0, other, rims)
    clean, noisy, tangent = [
        jnp.concatenate([f, first[i], second[i]], axis=0)
        for i, f in enumerate((volume, noise, cotangent))
    ]

    total = members * PPD
    all_corner, all_level = pick_patches(
        patch_count[0], patch_corner[0], patch_level[0], 0, total
    )
    group_first = group * heads * PPD
    corner = lax.dynamic_slice(all_corner, (group_first, 0), (heads * PPD, 3))
    level = lax.dynamic_slice(all_level, (group_first,), (heads * PPD,))
    corner = jnp.stack([corner[:, 0] - slab * planes, corner[:, 1] // 8, corner[:, 2]], axis=1)
    own_corner = lax.dynamic_slice(corner, (head * PPD, 0), (PPD, 3))
    levels = jnp.stack(
        [among_slabs(all_level, k) if k else all_level for k in range(slabs)]
    )
    levels = jnp.take(levels, jnp.arange(slabs, dtype=jnp.int32) ^ slab, axis=0).reshape(-1)
    onehot = (levels[:, None] == jnp.arange(level_table.shape[0], dtype=jnp.int32)[None, :]).astype(
        BF16
    )
    level_rows = jnp.dot(onehot, level_table, preferred_element_type=F32).astype(BF16)

    pos = pos_embed.reshape(PZT * PXY, PXY, width).transpose(1, 0, 2).reshape(TOK, width)

    sigma_level, factor = noise_factors(level)
    tokens = cut_tokens(corner, jnp.stack([sigma_level, factor], axis=1), (clean, noisy))
    tangents = cut_tokens(own_corner, jnp.zeros((PPD, 2), F32), (tangent,))

    own_tokens = lax.dynamic_slice(tokens, (head * PPD, 0, 0), (PPD, TOK, VOX))
    own_place = slab * total + member * PPD
    own_rows = lax.dynamic_slice(level_rows, (own_place, 0), (PPD, width)).astype(F32)
    hidden = jnp.dot(own_tokens.reshape(PPD * TOK, VOX), embed, preferred_element_type=F32)
    hidden = hidden.reshape(PPD, TOK, width) + own_rows[:, None, :] + pos.astype(F32)[None]
    centre = hidden - jnp.mean(hidden, axis=-1, keepdims=True)
    scale = lax.rsqrt(jnp.mean(centre * centre, axis=-1) + 1e-05)[None]
    step = 1
    while step < heads:
        scale = jnp.concatenate([scale, in_group(scale, step)], axis=0)
        step *= 2
    scales = [scale[:, n].reshape(heads, 1, TOK) for n in range(PPD)]

    fold = fold_weights(me, embed, pos, level_rows, w_blocks)
    folds = jnp.stack([among_slabs(fold, k) if k else fold for k in range(slabs)])
    full_out = lax.all_gather(w_out, "fsdp", axis=0, tiled=True)

    infos = [
        jnp.stack([head, slab * total + group_first + n] + [slab ^ j for j in range(KINDS)]).astype(
            jnp.int32
        )
        for n in range(PPD)
    ]
    head_me = jnp.reshape(head, (1,)).astype(jnp.int32)
    scores, wides, d_hiddens, d_atts = [], [], [], []
    for n in range(PPD):
        att = forward_heads(n, infos[n], tokens, scales[n], folds)
        attended = [in_group(att[k], k) if k else att[0] for k in range(heads)]
        score, wide, d_hidden, d_att = output_part(
            head_me, hidden[n], tangents[n], full_out, unembed, attended
        )
        scores.append(score)
        wides.append(wide)
        d_hiddens.append(d_hidden)
        d_atts.append(jnp.stack([in_group(d_att[k], k) if k else d_att[0] for k in range(heads)]))
    rows = fold.shape[0]
    sums = jnp.zeros((KINDS, rows, HD), F32)
    for n in range(PPD):
        sums = backward_heads(n, infos[n], tokens, scales[n], folds, d_atts[n], sums)
    sums = sums.astype(BF16)

    half = slabs // 2

    def sums_for(target):
        qk = lax.dynamic_index_in_dim(sums, target // half, 0, keepdims=False)
        return jnp.concatenate([qk, sums[2]], axis=1)

    others = [among_slabs(sums_for(slab ^ k), k) for k in range(1, slabs)]
    own = sums_for(slab)
    if groups > 1:
        gathered = own.astype(F32)
        for block in others:
            gathered += block.astype(F32)
        own = gathered.astype(BF16)
        others = [
            swap(own, "fsdp", [(i, ((i // heads) ^ g) * heads + i % heads) for i in range(members)])
            for g in range(1, groups)
        ]
    blocks = expand_sums(me, heads, depth, embed, pos, level_rows, own, others)
    qk_heads = heads // half
    v_heads = heads // slabs
    pairs_of = []
    for k in range(heads):
        pairs = []
        for s in range(slabs):
            for i in range(members):
                h = i % heads
                if h // qk_heads == s % half or h // v_heads == s:
                    j = (i // heads) * heads + (h ^ k)
                    pairs.append((s * members + i, s * members + j))
        pairs_of.append(pairs)
    arrived = jnp.stack(
        [swap(blocks[k], ("slab", "fsdp"), pairs_of[k]) if k else blocks[0] for k in range(heads)]
    )

    def from_heads(first, number, column):
        pieces = [
            lax.dynamic_index_in_dim(arrived, head ^ (first + i), 0, keepdims=False)[
                :, column * HD : (column + 1) * HD
            ]
            for i in range(number)
        ]
        return jnp.concatenate(pieces, axis=1).astype(F32)

    grad_qk = from_heads((slab % half) * qk_heads, qk_heads, 0)
    grad_v = from_heads(slab * v_heads, v_heads, 1)

    out_term = first_dot(
        jnp.concatenate(wides, axis=0), jnp.concatenate(d_hiddens, axis=0)
    ).astype(BF16)
    out_part = lax.psum_scatter(out_term, "fsdp", scatter_dimension=0, tiled=True)
    grad_out = lax.psum_scatter(out_part, "slab", scatter_dimension=1, tiled=True).astype(F32)

    buffer = place_scores(own_corner, scores, planes + HALO, side)
    summed = lax.psum_scatter(buffer, "fsdp", scatter_dimension=1, tiled=True)
    arrived_rim = swap(summed[planes:], "slab", [(i, i + 1) for i in range(slabs - 1)])
    score = summed[:planes].astype(F32).at[:HALO].add(arrived_rim.astype(F32))
    return (score, grad_qk, grad_v, grad_out)


def solution(mesh):
    placed = (
        P("slab", None, None),
        P("slab", None, None),
        P("slab", None, None),
        P("slab", None, None),
        P("slab", None),
        P("slab", None),
        P(),
        P(),
        P(),
        P(),
        P("fsdp", None),
        P("fsdp", None),
    )
    return jax.shard_map(
        functools.partial(on_device, mesh.shape["slab"], mesh.shape["fsdp"]),
        mesh=mesh,
        in_specs=placed,
        out_specs=(
            P("slab", "fsdp", None),
            P("fsdp", "slab"),
            P("fsdp", "slab"),
            P("fsdp", "slab"),
        ),
        check_vma=False,
    )
```

time: 531 us -> 383 us (0.72); the launches traced: 525 us -> 382 us
  local copies, waits for them, and re-layouts: 206 us -> 52.3 us
  Pallas kernels: 0 us -> 112 us
  starting transfers between devices: 7.96 us -> 84 us
  matrix products: 84.7 us -> 10.1 us
  waiting for transfers between devices: 169 us -> 96.7 us
  other arithmetic: 31.3 us -> 12.4 us
  between operations: 25.5 us -> 14.9 us
    reduce_scatter x7 -> x3, waiting for transfers between devices: 151 us -> 18.6 us  [the longest x1 18.6 us: on_device(): lax.psum_scatter(out_part, 'slab', scatter_dimension=1, tiled=True)]
    pallas_call x0 -> x11, Pallas kernels: none -> 112 us  [the longest x2 40.6 us: cut_tokens(): pl.pallas_call(functools.partial(cut_kernel, len(fields) == 2), grid=(cou...]
    ppermute x4 -> x57, starting transfers between devices: 7.42 us -> 83.6 us  [the longest x40 63.8 us: swap(): return lax.ppermute(block, axis, pairs)]
    dot_general x16 -> x3, matrix products: 84.7 us -> 10.1 us  [the longest x1 4.43 us: first_dot(): lax.dot_general(left, right, (((0,), (0,)), ((), ())), preferred_element_...]
    ppermute x4 -> x57, waiting for transfers between devices: 7.13 us -> 78 us  [the longest x40 45.2 us: swap(): return lax.ppermute(block, axis, pairs)]
    convert_element_type x10 -> x0, local copies, waits for them, and re-layouts: 42.5 us -> none  [the longest x6 34.5 us: cut_patches(): token_list.append(to_tokens(field * factor[number]).astype(jnp.bfloat16))]
    transpose x4 -> x0, local copies, waits for them, and re-layouts: 34 us -> none  [the longest x2 23.3 us: from_tokens(): token_rows.reshape(PZT, PXY, PXY, EDGE, EDGE, EDGE)]
    dynamic_update_slice x2 -> x0, local copies, waits for them, and re-layouts: 26.1 us -> none  [place_scores(): buffer = lax.dynamic_update_slice(buffer, block, starts)]
  transfers between devices with their start and end apart: 13 -> 61, of which waited for: 8 -> 16; matrix products, arithmetic and copies ran while one was open for 54% -> 12% of each run, Pallas kernels for 0% -> 27%
where the time goes in v1:
time: 383 us; the launch traced here: 382 us
  Pallas kernels  112 us (29%)
  waiting for transfers between devices  96.7 us (25%)
  starting transfers between devices  84 us (22%)
  local copies, waits for them, and re-layouts  52.3 us (14%)
  between operations  14.9 us (4%)
  other arithmetic  12.4 us (3%)
  matrix products  10.1 us (3%)
    ppermute x40, starting transfers between devices, swap(): return lax.ppermute(block, axis, pairs)  63.8 us
    ppermute x40, waiting for transfers between devices, swap(): return lax.ppermute(block, axis, pairs)  45.2 us
    pallas_call x2, Pallas kernels, cut_tokens(): pl.pallas_call(functools.partial(cut_kernel, len(fields) == 2), grid=(cou...  40.6 us
    ppermute x17, waiting for transfers between devices, across(): return lax.ppermute(block, axis, [(i, i ^ k) for i in range(size)])  32.8 us
    unnamed x123, local copies, waits for them, and re-layouts  31.2 us
    pallas_call x2, Pallas kernels, backward_heads(): pl.pallas_call(backward_kernel, grid_spec=pltpu.PrefetchScalarGridSpec(nu...  30.6 us
    ppermute x17, starting transfers between devices, across(): return lax.ppermute(block, axis, [(i, i ^ k) for i in range(size)])  19.8 us
    reduce_scatter x1, waiting for transfers between devices, on_device(): lax.psum_scatter(out_part, 'slab', scatter_dimension=1, tiled=True)  18.6 us
  transfers between devices with their start and end apart: 61, of which 16 were waited for; matrix products, arithmetic and copies ran while one was open for 12% of the time, Pallas kernels for 27%

profile of v1, /device:TPU:0, one launch (start us, length us, event | category | flops | bytes accessed | tf_op | source)
XLA Modules:
  0.0 381.9 jit_solution(7673592500475309884)
XLA Ops:
  23.0 25.1 %collective-permute-done = bf16[3,12,128,128]{3,2,1,0:T(8,128)(2,1)} collective-permute-done((bf16[3,12,128,128]{3,2,1,0:T(8,128)(2,1)S(1)}, bf16[3,12,128,128]{3,2,1,0:T(8,128)(2,1)}, u32[]{:S(2)}, u32[]{:S(2)}) %collective-permute-start) | collective-permute-done | bytes 1179680 | tf_op jit(solution)/shard_map/ppermute | solution.py:30
  51.2 3.4 collective-permute-start.13
  55.3 3.2 convolution_convert_fusion.1.level_ref
  59.2 3.8 collective-permute-done.11.refs_4_
  63.0 5.6 %collective-permute-done.12.refs_5_ = bf16[256,128]{1,0:T(8,128)(2,1)S(1)} collective-permute-done((bf16[256,128]{1,0:T(8,128)(2,1)S(1)}, bf16[256,128]{1,0:T(8,128)(2,1)S(1)}, u32[]{:S(2)}, u32[]{:S(2)}) %collective-permute-start.12) | collective-permute-done | bytes 65568 | tf_op jit(solution)/shard_map/ppermute | solution.py:34
  69.1 4.0 %collective-permute-done.9.refs_2_ = bf16[256,128]{1,0:T(8,128)(2,1)S(1)} collective-permute-done((bf16[256,128]{1,0:T(8,128)(2,1)S(1)}, bf16[256,128]{1,0:T(8,128)(2,1)S(1)}, u32[]{:S(2)}, u32[]{:S(2)}) %collective-permute-start.9) | collective-permute-done | bytes 65568 | tf_op jit(solution)/shard_map/ppermute | solution.py:34
  83.0 37.3 %cut_tokens.2.token_ref = bf16[16,256,512]{2,1,0:T(8,128)(2,1)} custom-call(s32[16,3]{1,0:T(8,128)S(1)} %copy.35.corner_ref, f32[16,2]{1,0:T(8,128)S(1)} %copy.37.factor_ref, bf16[56,16,8,128]{3,2,1,0:T(8,128)(2,1)S(1)} %pad_maximum_fusion.refs_0_, bf16[56,16,8,128]{3,2,1,0:T(8,128)(2,1)S(1)} %pad_maximum_fusion.1.refs_1_), custom_call_target="tpu_custom_call" | custom-call | tf_op jit(solution)/shard_map/cut_tokens/pallas_call | solution.py:126
  126.9 3.4 collective-permute-start.6
  135.4 4.8 %slice_bitcast_fusion = (f32[256,2048]{1,0:T(8,128)}, f32[256,2048]{1,0:T(8,128)}) fusion(f32[2,256,2048]{2,1,0:T(8,128)} %copy-done.42), kind=kLoop, calls=%fused_computation.5 | loop fusion | bytes 8388608 | tf_op jit(solution)/shard_map/squeeze | solution.py:531
  140.3 7.4 %forward_heads.3 = bf16[8,256,128]{2,1,0:T(8,128)(2,1)S(1)} custom-call(s32[5]{0:T(128)S(1)} %stack.172.info_ref, bf16[16,256,512]{2,1,0:T(8,128)(2,1)S(1)} %copy-done, f32[8,1,256]{2,1,0:T(1,128)S(1)} %get-tuple-element.107.scale_ref, bf16[4,832,128]{2,1,0:T(8,128)(2,1)S(1)} %pad_maximum_fusion.4.q_ref.k_ref.v_ref, ...), custom_call_target="tpu_custom_call" | custom-call | tf_op jit(solution)/shard_map/forward_heads/pallas_call | solution.py:304
  152.8 7.4 %forward_heads.2 = bf16[8,256,128]{2,1,0:T(8,128)(2,1)S(1)} custom-call(s32[5]{0:T(128)S(1)} %stack.165.info_ref, bf16[16,256,512]{2,1,0:T(8,128)(2,1)S(1)} %copy-done, f32[8,1,256]{2,1,0:T(1,128)S(1)} %get-tuple-element.108.scale_ref, bf16[4,832,128]{2,1,0:T(8,128)(2,1)S(1)} %pad_maximum_fusion.4.q_ref.k_ref.v_ref, ...), custom_call_target="tpu_custom_call" | custom-call | tf_op jit(solution)/shard_map/forward_heads/pallas_call | solution.py:304
  165.2 3.3 cut_tokens.3
  189.5 7.6 %output_part.3 = (f32[256,512]{1,0:T(8,128)S(1)}, bf16[256,1024]{1,0:T(8,128)(2,1)S(1)}, bf16[256,2048]{1,0:T(8,128)(2,1)S(1)}, bf16[8,256,128]{2,1,0:T(8,128)(2,1)S(1)}) custom-call(s32[1]{0:T(128)} %bitcast.1.me_ref, f32[256,2048]{1,0:T(8,128)S(1)} %copy-done.6, bf16[256,512]{1,0:T(8,128)(2,1)S(1)} %copy-done.8, ...), custom_call_target="tpu_custom_call" | custom-call | tf_op jit(solution)/shard_map/output_part/pallas_call | solution.py:367
  198.0 7.6 %output_part.2 = (f32[256,512]{1,0:T(8,128)S(1)}, bf16[256,1024]{1,0:T(8,128)(2,1)S(1)}, bf16[256,2048]{1,0:T(8,128)(2,1)S(1)}, bf16[8,256,128]{2,1,0:T(8,128)(2,1)S(1)}) custom-call(s32[1]{0:T(128)} %bitcast.1.me_ref, f32[256,2048]{1,0:T(8,128)S(1)} %copy-done.5, bf16[256,512]{1,0:T(8,128)(2,1)S(1)} %get-tuple-element.94.cot_ref, ...), custom_call_target="tpu_custom_call" | custom-call | tf_op jit(solution)/shard_map/output_part/pallas_call | solution.py:367
  207.2 4.4 %convolution_convert_fusion = bf16[1024,2048]{1,0:T(8,128)(2,1)} fusion(bf16[256,2048]{1,0:T(8,128)(2,1)S(1)} %get-tuple-element.31, bf16[256,2048]{1,0:T(8,128)(2,1)S(1)} %get-tuple-element.30, bf16[256,1024]{1,0:T(8,128)(2,1)S(1)} %get-tuple-element.29, bf16[256,1024]{1,0:T(8,128)(2,1)S(1)} %get-tuple-element.28), kind=kOutput, calls=%fused_computation.3 | convolution fusion | flops 2155872256 | bytes 7340032 | tf_op jit(solution)/shard_map/dot_general | solution.py:46
  220.8 7.2 %place_scores.1 = bf16[56,16,8,128]{3,2,1,0:T(8,128)(2,1)S(1)} custom-call(s32[2,3]{1,0:T(2,128)S(1)} %copy-done.37, f32[256,512]{1,0:T(8,128)S(1)} %copy-done.16, f32[256,512]{1,0:T(8,128)S(1)} %copy-done.14), custom_call_target="tpu_custom_call" | custom-call | tf_op jit(solution)/shard_map/place_scores/pallas_call | solution.py:173
  255.0 5.2 %collective-permute-done.37 = bf16[256,128]{1,0:T(8,128)(2,1)S(1)} collective-permute-done((bf16[256,128]{1,0:T(8,128)(2,1)S(1)}, bf16[256,128]{1,0:T(8,128)(2,1)S(1)}, u32[]{:S(2)}, u32[]{:S(2)}) %collective-permute-start.37) | collective-permute-done | bytes 65568 | tf_op jit(solution)/shard_map/ppermute | solution.py:30
  261.7 15.3 %backward_heads.2.last_ref = f32[3,832,128]{2,1,0:T(8,128)S(1)} custom-call(s32[5]{0:T(128)S(1)} %copy-done.41, bf16[16,256,512]{2,1,0:T(8,128)(2,1)} %cut_tokens.2.token_ref, f32[8,1,256]{2,1,0:T(1,128)S(1)} %get-tuple-element.108.scale_ref, bf16[4,832,128]{2,1,0:T(8,128)(2,1)S(1)} %pad_maximum_fusion.4.q_ref.k_ref.v_ref, ...), custom_call_target="tpu_custom_call" | custom-call | tf_op jit(solution)/shard_map/backward_heads/pallas_call | solution.py:322
  277.0 15.3 %backward_heads.3 = f32[3,832,128]{2,1,0:T(8,128)S(1)} custom-call(s32[5]{0:T(128)S(1)} %copy-done.39, bf16[16,256,512]{2,1,0:T(8,128)(2,1)} %cut_tokens.2.token_ref, f32[8,1,256]{2,1,0:T(1,128)S(1)} %get-tuple-element.107.scale_ref, bf16[4,832,128]{2,1,0:T(8,128)(2,1)S(1)} %pad_maximum_fusion.4.q_ref.k_ref.v_ref, ...), custom_call_target="tpu_custom_call" | custom-call | tf_op jit(solution)/shard_map/backward_heads/pallas_call | solution.py:322
  296.2 9.1 %collective-permute-done.47.refs_0_ = bf16[832,256]{1,0:T(8,128)(2,1)S(1)} collective-permute-done((bf16[832,256]{1,0:T(8,128)(2,1)S(1)}, bf16[832,256]{1,0:T(8,128)(2,1)S(1)}, u32[]{:S(2)}, u32[]{:S(2)}) %collective-permute-start.47) | collective-permute-done | bytes 426016 | tf_op jit(solution)/shard_map/ppermute | solution.py:34
  305.3 10.3 %collective-permute-done.48.refs_1_ = bf16[832,256]{1,0:T(8,128)(2,1)S(1)} collective-permute-done((bf16[832,256]{1,0:T(8,128)(2,1)S(1)}, bf16[832,256]{1,0:T(8,128)(2,1)S(1)}, u32[]{:S(2)}, u32[]{:S(2)}) %collective-permute-start.48) | collective-permute-done | bytes 426016 | tf_op jit(solution)/shard_map/ppermute | solution.py:34
  319.4 5.9 %collective-permute-start.51 = (bf16[256,256]{1,0:T(8,128)(2,1)S(1)}, bf16[256,256]{1,0:T(8,128)(2,1)S(1)}, u32[]{:S(2)}, u32[]{:S(2)}) collective-permute-start(bf16[256,256]{1,0:T(8,128)(2,1)S(1)} %get-tuple-element.61), channel_id=1, source_target_pairs={{0,2},{1,3},{2,0},{3,1},{10,8},{11,9},{12,14},{13,15},{14,12},{15,... | collective-permute-start | bytes 393224 | tf_op jit(solution)/shard_map/ppermute | solution.py:30
  345.5 7.0 %collective-permute-start.32 = (bf16[24,16,128]{2,1,0:T(8,128)(2,1)S(1)}, bf16[24,16,128]{2,1,0:T(8,128)(2,1)S(1)}, u32[]{:S(2)}, u32[]{:S(2)}) collective-permute-start(bf16[24,16,128]{2,1,0:T(8,128)(2,1)S(1)} %slice.316), channel_id=1, source_target_pairs={{0,8},{8,16},{16,24},{1,9},{9,17},{17,25},{2,10},{10,18},{18,26},{... | collective-permute-start | bytes 294920 | tf_op jit(solution)/shard_map/ppermute | solution.py:30
  355.2 18.6 %reduce-scatter.8.cloned.1.call-done = bf16[128,512]{1,0:T(8,128)(2,1)} async-done(((bf16[128,2048]{1,0:T(8,128)(2,1)}), bf16[128,512]{1,0:T(8,128)(2,1)}) %reduce-scatter.8.cloned.1.call-update) | async-done | bytes 131088 | tf_op jit(solution)/shard_map/reduce_scatter | solution.py:593
  (315 shorter events, 144.8 us)
Async XLA Ops:
  7.2 173.1 %all-gather.2.cloned.1.call-start = ((), (), s32[]{:S(2)}) async-start(), calls=%async_computation.3 | async-start | bytes 4718592 | tf_op jit(solution)/shard_map/all_gather | solution.py:517
  9.1 39.7 %collective-permute-start.2 = (s32[16]{0:T(128)S(1)}, s32[16]{0:T(128)S(1)}, u32[]{:S(2)}, u32[]{:S(2)}) collective-permute-start(s32[16]{0:T(128)S(1)} %select_reduce_fusion), channel_id=1, source_target_pairs={{0,8},{8,0},{16,24},{24,16},{1,9},{9,1},{17,25},{25,17},{2,10},{10... | collective-permute-start | bytes 200 | tf_op jit(solution)/shard_map/ppermute | solution.py:34
  12.1 39.1 %collective-permute-start.3 = (s32[16]{0:T(128)S(1)}, s32[16]{0:T(128)S(1)}, u32[]{:S(2)}, u32[]{:S(2)}) collective-permute-start(s32[16]{0:T(128)S(1)} %select_reduce_fusion), channel_id=1, source_target_pairs={{0,16},{8,24},{16,0},{24,8},{1,17},{9,25},{17,1},{25,9},{2,18},{10... | collective-permute-start | bytes 200 | tf_op jit(solution)/shard_map/ppermute | solution.py:34
  13.6 37.6 %collective-permute-start.4 = (s32[16]{0:T(128)S(1)}, s32[16]{0:T(128)S(1)}, u32[]{:S(2)}, u32[]{:S(2)}) collective-permute-start(s32[16]{0:T(128)S(1)} %select_reduce_fusion), channel_id=1, source_target_pairs={{0,24},{8,16},{16,8},{24,0},{1,25},{9,17},{17,9},{25,1},{2,26},{10... | collective-permute-start | bytes 200 | tf_op jit(solution)/shard_map/ppermute | solution.py:34
  14.7 43.8 %collective-permute-start.10 = (bf16[256,128]{1,0:T(8,128)(2,1)S(1)}, bf16[256,128]{1,0:T(8,128)(2,1)S(1)}, u32[]{:S(2)}, u32[]{:S(2)}) collective-permute-start(bf16[256,128]{1,0:T(8,128)(2,1)S(1)} %get-tuple-element.39), channel_id=1, source_target_pairs={{0,3},{1,2},{2,1},{3,0},{4,7},{5,6},{6,5},{7,4},{8,11},{9,10},{10,... | collective-permute-start | bytes 196616 | tf_op jit(solution)/shard_map/ppermute | solution.py:34
  17.8 30.4 %collective-permute-start = (bf16[3,12,128,128]{3,2,1,0:T(8,128)(2,1)S(1)}, bf16[3,12,128,128]{3,2,1,0:T(8,128)(2,1)}, u32[]{:S(2)}, u32[]{:S(2)}) collective-permute-start(bf16[3,12,128,128]{3,2,1,0:T(8,128)(2,1)S(1)} %pad_maximum_fusion.3), channel_id=1, source_target_pairs={{8,0},{16,8},{24,16},{9,1},{17,9},{25,17},{10,2},{18,10},{26,18},{... | collective-permute-start | bytes 3538952 | tf_op jit(solution)/shard_map/ppermute | solution.py:30
  19.1 321.4 %reduce-scatter.6.cloned.1.call-start = ((), (), s32[]{:S(2)}) async-start(), calls=%async_computation.5 | async-start | bytes 4718592 | tf_op jit(solution)/shard_map/reduce_scatter | solution.py:592
  48.1 29.9 %collective-permute-start.1 = (bf16[3,12,128,128]{3,2,1,0:T(8,128)(2,1)}, bf16[3,12,128,128]{3,2,1,0:T(8,128)(2,1)}, u32[]{:S(2)}, u32[]{:S(2)}) collective-permute-start(bf16[3,12,128,128]{3,2,1,0:T(8,128)(2,1)} %collective-permute-done), channel_id=1, source_target_pairs={{0,1},{1,0},{2,3},{3,2},{4,5},{5,4},{6,7},{7,6},{8,9},{9,8},{10,11... | collective-permute-start | bytes 3538952 | tf_op jit(solution)/shard_map/ppermute | solution.py:34
  74.5 55.8 %collective-permute-start.15 = (bf16[832,128]{1,0:T(8,128)(2,1)S(1)}, bf16[832,128]{1,0:T(8,128)(2,1)S(1)}, u32[]{:S(2)}, u32[]{:S(2)}) collective-permute-start(bf16[832,128]{1,0:T(8,128)(2,1)S(1)} %fold_weights.1), channel_id=1, source_target_pairs={{0,8},{8,0},{16,24},{24,16},{1,9},{9,1},{17,25},{25,17},{2,10},{10... | collective-permute-start | bytes 638984 | tf_op jit(solution)/shard_map/ppermute | solution.py:34
  75.7 54.6 %collective-permute-start.16 = (bf16[832,128]{1,0:T(8,128)(2,1)S(1)}, bf16[832,128]{1,0:T(8,128)(2,1)}, u32[]{:S(2)}, u32[]{:S(2)}) collective-permute-start(bf16[832,128]{1,0:T(8,128)(2,1)S(1)} %fold_weights.1), channel_id=1, source_target_pairs={{0,16},{8,24},{16,0},{24,8},{1,17},{9,25},{17,1},{25,9},{2,18},{10... | collective-permute-start | bytes 638984 | tf_op jit(solution)/shard_map/ppermute | solution.py:34
  75.9 54.4 %collective-permute-start.17 = (bf16[832,128]{1,0:T(8,128)(2,1)S(1)}, bf16[832,128]{1,0:T(8,128)(2,1)}, u32[]{:S(2)}, u32[]{:S(2)}) collective-permute-start(bf16[832,128]{1,0:T(8,128)(2,1)S(1)} %fold_weights.1), channel_id=1, source_target_pairs={{0,24},{8,16},{16,8},{24,0},{1,25},{9,17},{17,9},{25,1},{2,26},{10... | collective-permute-start | bytes 638984 | tf_op jit(solution)/shard_map/ppermute | solution.py:34
  169.3 28.7 %collective-permute-start.20 = (bf16[256,128]{1,0:T(8,128)(2,1)}, bf16[256,128]{1,0:T(8,128)(2,1)}, u32[]{:S(2)}, u32[]{:S(2)}) collective-permute-start(bf16[256,128]{1,0:T(8,128)(2,1)} %get-tuple-element.99), channel_id=1, source_target_pairs={{0,3},{1,2},{2,1},{3,0},{4,7},{5,6},{6,5},{7,4},{8,11},{9,10},{10,... | collective-permute-start | bytes 196616 | tf_op jit(solution)/shard_map/ppermute | solution.py:30
  171.4 26.5 %collective-permute-start.21 = (bf16[256,128]{1,0:T(8,128)(2,1)}, bf16[256,128]{1,0:T(8,128)(2,1)}, u32[]{:S(2)}, u32[]{:S(2)}) collective-permute-start(bf16[256,128]{1,0:T(8,128)(2,1)} %get-tuple-element.98), channel_id=1, source_target_pairs={{0,4},{1,5},{2,6},{3,7},{4,0},{5,1},{6,2},{7,3},{8,12},{9,13},{10,... | collective-permute-start | bytes 196616 | tf_op jit(solution)/shard_map/ppermute | solution.py:30
  172.5 25.5 %collective-permute-start.22 = (bf16[256,128]{1,0:T(8,128)(2,1)}, bf16[256,128]{1,0:T(8,128)(2,1)}, u32[]{:S(2)}, u32[]{:S(2)}) collective-permute-start(bf16[256,128]{1,0:T(8,128)(2,1)} %get-tuple-element.97), channel_id=1, source_target_pairs={{0,5},{1,4},{2,7},{3,6},{4,1},{5,0},{6,3},{7,2},{8,13},{9,12},{10,... | collective-permute-start | bytes 196616 | tf_op jit(solution)/shard_map/ppermute | solution.py:30
  175.5 22.4 %collective-permute-start.23 = (bf16[256,128]{1,0:T(8,128)(2,1)}, bf16[256,128]{1,0:T(8,128)(2,1)}, u32[]{:S(2)}, u32[]{:S(2)}) collective-permute-start(bf16[256,128]{1,0:T(8,128)(2,1)} %get-tuple-element.96), channel_id=1, source_target_pairs={{0,6},{1,7},{2,4},{3,5},{4,2},{5,3},{6,0},{7,1},{8,14},{9,15},{10,... | collective-permute-start | bytes 196616 | tf_op jit(solution)/shard_map/ppermute | solution.py:30
  177.6 20.4 %collective-permute-start.24 = (bf16[256,128]{1,0:T(8,128)(2,1)}, bf16[256,128]{1,0:T(8,128)(2,1)}, u32[]{:S(2)}, u32[]{:S(2)}) collective-permute-start(bf16[256,128]{1,0:T(8,128)(2,1)} %get-tuple-element.95), channel_id=1, source_target_pairs={{0,7},{1,6},{2,5},{3,4},{4,3},{5,2},{6,1},{7,0},{8,15},{9,14},{10,... | collective-permute-start | bytes 196616 | tf_op jit(solution)/shard_map/ppermute | solution.py:30
  211.7 132.9 %reduce-scatter.4.cloned.1.call-start = ((), (), s32[]{:S(2)}) async-start(), calls=%async_computation.4 | async-start | bytes 2064384 | tf_op jit(solution)/shard_map/reduce_scatter | solution.py:596
  214.6 21.0 %collective-permute-start.42 = (bf16[256,128]{1,0:T(8,128)(2,1)}, bf16[256,128]{1,0:T(8,128)(2,1)}, u32[]{:S(2)}, u32[]{:S(2)}) collective-permute-start(bf16[256,128]{1,0:T(8,128)(2,1)} %get-tuple-element.73), channel_id=1, source_target_pairs={{0,3},{1,2},{2,1},{3,0},{4,7},{5,6},{6,5},{7,4},{8,11},{9,10},{10,... | collective-permute-start | bytes 196616 | tf_op jit(solution)/shard_map/ppermute | solution.py:30
  216.0 21.7 %collective-permute-start.43 = (bf16[256,128]{1,0:T(8,128)(2,1)}, bf16[256,128]{1,0:T(8,128)(2,1)}, u32[]{:S(2)}, u32[]{:S(2)}) collective-permute-start(bf16[256,128]{1,0:T(8,128)(2,1)} %get-tuple-element.72), channel_id=1, source_target_pairs={{0,4},{1,5},{2,6},{3,7},{4,0},{5,1},{6,2},{7,3},{8,12},{9,13},{10,... | collective-permute-start | bytes 196616 | tf_op jit(solution)/shard_map/ppermute | solution.py:30
  216.6 22.6 %collective-permute-start.44 = (bf16[256,128]{1,0:T(8,128)(2,1)}, bf16[256,128]{1,0:T(8,128)(2,1)}, u32[]{:S(2)}, u32[]{:S(2)}) collective-permute-start(bf16[256,128]{1,0:T(8,128)(2,1)} %get-tuple-element.71), channel_id=1, source_target_pairs={{0,5},{1,4},{2,7},{3,6},{4,1},{5,0},{6,3},{7,2},{8,13},{9,12},{10,... | collective-permute-start | bytes 196616 | tf_op jit(solution)/shard_map/ppermute | solution.py:30
  229.3 144.5 %reduce-scatter.8.cloned.1.call-start = ((), (), s32[]{:S(2)}) async-start(), calls=%async_computation.6 | async-start | bytes 655360 | tf_op jit(solution)/shard_map/reduce_scatter | solution.py:593
  248.5 28.5 %collective-permute-start.39 = (bf16[256,128]{1,0:T(8,128)(2,1)S(1)}, bf16[256,128]{1,0:T(8,128)(2,1)S(1)}, u32[]{:S(2)}, u32[]{:S(2)}) collective-permute-start(bf16[256,128]{1,0:T(8,128)(2,1)S(1)} %get-tuple-element.77), channel_id=1, source_target_pairs={{0,7},{1,6},{2,5},{3,4},{4,3},{5,2},{6,1},{7,0},{8,15},{9,14},{10,... | collective-permute-start | bytes 196616 | tf_op jit(solution)/shard_map/ppermute | solution.py:30
  294.7 20.9 %collective-permute-start.48 = (bf16[832,256]{1,0:T(8,128)(2,1)S(1)}, bf16[832,256]{1,0:T(8,128)(2,1)S(1)}, u32[]{:S(2)}, u32[]{:S(2)}) collective-permute-start(bf16[832,256]{1,0:T(8,128)(2,1)S(1)} %get-tuple-element.105), channel_id=1, source_target_pairs={{0,16},{8,24},{16,0},{24,8},{1,17},{9,25},{17,1},{25,9},{2,18},{10... | collective-permute-start | bytes 1277960 | tf_op jit(solution)/shard_map/ppermute | solution.py:34
  294.7 20.9 %collective-permute-start.49 = (bf16[832,256]{1,0:T(8,128)(2,1)S(1)}, bf16[832,256]{1,0:T(8,128)(2,1)S(1)}, u32[]{:S(2)}, u32[]{:S(2)}) collective-permute-start(bf16[832,256]{1,0:T(8,128)(2,1)S(1)} %get-tuple-element.103), channel_id=1, source_target_pairs={{0,24},{8,16},{16,8},{24,0},{1,25},{9,17},{17,9},{25,1},{2,26},{10... | collective-permute-start | bytes 1277960 | tf_op jit(solution)/shard_map/ppermute | solution.py:34
  (89 other events, 848.3 us)
Sparse Core Ops, SparseCore 0:
  19.2 61.5 all-gather.1
  211.8 67.4 reduce-scatter.5
  281.6 37.6 reduce-scatter.3
  340.6 33.0 reduce-scatter.7
